TPU v7x, 1024 devices: a whole 4x8x16 slice. The times are simulated.
1024 devices in a mesh: blk: 128 (over z, y), line: 8 (over x, core).
Axes of the slice: x: 4, y: 8, z: 16, core: 2. Of those that a mesh axis runs over, the one named last changes fastest.
Arguments:
- flow_state: float32 [128, 5, 512, 512], P('blk', None, 'line'), may hold values from -6 to 6
- block_owner: int32 [128], replicated, may hold values from 0 to 127, each once
- link_block: int32 [128, 2], replicated, may hold values from 0 to 127, as said below
- link_side: int32 [128, 2], replicated, may hold values from 0 to 1
- rows_live: int32 [128], replicated, may hold values from 256 to 512, as said below
- x_operator: float32 [512, 1024], replicated, may hold values from -0.25 to 0.25
- ghost_operator: float32 [6, 1024], replicated, may hold values from -1.25 to 1.25
- y_operator: float32 [512, 1024], replicated, may hold values from -0.25 to 0.25
- coefficients: float32 [7], replicated, may hold values from 0.2 to 1
Outputs:
- next_state: float32 [128, 5, 512, 512], P('blk', None, 'line')
Inputs may be any that keep to these rules, and one draw needn't show every extreme that they name: link_block and link_side join the blocks' faces in pairs: if face m of block b meets face s of block c, then face s of block c meets face m of block b; no block meets itself. `rows_live`: some block has all 512 lines.
All inputs are finite; a program needn't handle non-finite values.
Results may differ from a plain program's by a relative error of at most 0.0003.
Values sent between devices are 32-bit elements; how exact they have to be, the bound alone decides.
A program may use at most 32 MiB of HBM per device.

v0:
```python
import jax
import jax.numpy as jnp
from jax import lax
from jax.sharding import PartitionSpec as P

GHOST = 3


highest = lax.Precision.HIGHEST
section_step = 0.3


def on_device(
    flow_state,
    block_owner,
    link_block,
    link_side,
    rows_live,
    x_operator,
    ghost_operator,
    y_operator,
    coefficients,
):
    values = flow_state[0]
    var_count, rows_here, x_length = values.shape
    my_slot = lax.axis_index("blk")
    line_pos = lax.axis_index("line")
    block_count = block_owner.shape[0]
    numbers = jnp.arange(block_count, dtype=jnp.int32)
    my_block = jnp.sum(numbers * (block_owner == my_slot).astype(jnp.int32))
    block_pick = (numbers == my_block).astype(jnp.int32)
    live_rows = jnp.sum(rows_live * block_pick)
    y_index = line_pos * rows_here + jnp.arange(rows_here, dtype=jnp.int32)
    live_mask = (y_index < live_rows).astype(jnp.float32)
    masked = values * live_mask[None, :, None]
    low_planes = jnp.swapaxes(masked[:, :, :GHOST], 1, 2)
    high_planes = jnp.swapaxes(masked[:, :, x_length - GHOST :], 1, 2)
    face_planes = jnp.stack([low_planes, high_planes], axis=1)[None]
    neighbours = jnp.sum(link_block * block_pick[:, None], axis=0)
    their_sides = jnp.sum(link_side * block_pick[:, None], axis=0)
    sources = jnp.sum(
        block_owner[None, :] * (numbers[None, :] == neighbours[:, None]).astype(jnp.int32), axis=1
    )
    shard_piece = lax.all_gather(face_planes, "blk", axis=0, tiled=True)
    row_ids = jnp.arange(shard_piece.shape[0], dtype=jnp.int32)
    select = (row_ids[None, :] == sources[:, None]).astype(jnp.float32)
    received = jnp.einsum("mn,nvsgy->mvsgy", select, shard_piece, precision=highest)
    flip_sign = jnp.array([-1.0, 1.0, 1.0, 1.0, 1.0], jnp.float32)[:, None, None]
    side_ghosts = []
    for my_side in range(2):
        far_side = their_sides[my_side]
        chosen = jnp.where(far_side == 0, received[my_side, :, 0], received[my_side, :, 1])
        side_ghosts.append(jnp.where(far_side == my_side, chosen[:, ::-1] * flip_sign, chosen))
    ghost_planes = jnp.concatenate(side_ghosts, axis=1)
    nu_values = coefficients[:var_count][:, None, None]
    x_parts = jnp.einsum("vyx,xk->vyk", masked, x_operator, precision=highest)
    x_parts = x_parts + jnp.einsum("vgy,gk->vyk", ghost_planes, ghost_operator, precision=highest)
    x_term = -masked[0][None] * x_parts[..., :x_length] + nu_values * x_parts[..., x_length:]
    columns = lax.all_to_all(masked, "line", split_axis=2, concat_axis=1, tiled=True)
    y_full = columns.shape[1]
    y_parts = jnp.einsum("vyx,yk->vxk", columns, y_operator, precision=highest)
    v_columns = jnp.swapaxes(columns[1], 0, 1)
    y_cols_term = -v_columns[None] * y_parts[..., :y_full] + nu_values * y_parts[..., y_full:]
    y_rows = lax.all_to_all(y_cols_term, "line", split_axis=2, concat_axis=1, tiled=True)
    y_term = jnp.swapaxes(y_rows, 1, 2)
    buoyancy = coefficients[var_count] * masked[3] + coefficients[var_count + 1] * masked[4]
    picker = (jnp.arange(var_count) == 1).astype(jnp.float32)[:, None, None]
    rhs_terms = x_term + y_term + picker * buoyancy[None]
    result = (masked + section_step * rhs_terms) * live_mask[None, :, None]
    return result[None]


def solution(mesh):
    return jax.shard_map(
        on_device,
        mesh=mesh,
        in_specs=(P("blk", None, "line", None), P(), P(), P(), P(), P(), P(), P(), P()),
        out_specs=P("blk", None, "line", None),
        check_vma=False,
    )
```

profile of v0, /device:TPU:1, one launch (start us, length us, event | category | flops | bytes accessed | tf_op | source)
XLA Modules:
  0.0 190.0 jit_solution(1614993829590794076)
XLA Ops:
  0.0 0.0 copy-start
  0.0 1.4 fusion.31
  1.5 1.9 %fusion.30 = s32[]{:T(128)} fusion(s32[128]{0:T(128)} %param.14, s32[]{:T(128)} %fusion.31), kind=kLoop, calls=%fused_computation.55 | loop fusion | flops 383 | bytes 520 | tf_op jit(solution)/shard_map/reduce_sum | solution.py:32
  3.4 0.6 compare_convert_fusion.1
  4.0 1.2 bitcast_multiply_fusion
  5.2 2.0 %copy.52 = f32[5,64,512]{1,0,2:T(8,128)} copy(f32[5,64,512]{2,1,0:T(8,128)S(1)} %bitcast_multiply_fusion) | data formatting | bytes 1310720 | tf_op jit(solution)/shard_map/mul | solution.py:35
  7.2 3.1 %reshape.41 = f32[8,1,20480]{2,1,0:T(1,128)} reshape(f32[512,5,64]{2,1,0:T(8,128)} %bitcast.80) | data formatting | bytes 1310720
  10.3 17.6 %all-to-all-start = ((f32[8,1,20480]{2,1,0:T(1,128)}), f32[8,1,20480]{2,1,0:T(1,128)S(1)}, u32[]{:S(2)}, u32[]{:S(2)}) async-start(f32[8,1,20480]{2,1,0:T(1,128)} %reshape.41), calls=%async_computation | async-start | bytes 1310720 | tf_op jit(solution)/shard_map/all_to_all | solution.py:59
  27.9 0.6 compare_convert_fusion.2
  28.5 0.8 slice_bitcast_fusion.1
  29.3 0.0 copy-done.4
  29.3 0.1 multiply_reduce_fusion
  29.5 0.2 fusion.28
  29.6 0.6 fusion.36
  32.1 0.6 fusion.35
  32.7 1.0 copy.47
  33.7 1.0 copy.48
  34.8 0.0 copy-start.6
  34.8 0.0 copy-start.2
  34.8 80.2 %all-gather = f32[640,2,3,64]{3,1,2,0:T(2,128)S(1)} all-gather(f32[5,2,3,64]{3,1,2,0:T(2,128)S(1)} %pad_maximum_fusion), channel_id=2, replica_groups=mesh['blk'=128,'line'=8] {'blk'}, dimensions={0}, use_global_device_ids=true | all-gather | bytes 990720 | tf_op jit(solution)/shard_map/all_gather | solution.py:44
  115.0 0.8 fusion.4
  115.9 0.0 copy-done.6
  115.9 0.1 multiply_select_fusion.1
  116.0 0.0 copy-done.2
  116.0 2.3 %fusion.20 = f32[5,64,1024]{2,1,0:T(8,128)} fusion(f32[6,1024]{1,0:T(8,128)S(1)} %copy-done.2, f32[5,3,64]{2,1,0:T(4,128)S(1)} %get-tuple-element.17, f32[5,3,64]{2,1,0:T(4,128)S(1)} %get-tuple-element.16), kind=kOutput, calls=%fused_computation.31 | convolution fusion | flops 23594880 | bytes 1342976 | tf_op jit(solution)/shard_map/vgy,gk->vyk/dot_general | solution.py:57
  118.3 0.0 all-to-all-done
  118.3 0.5 broadcast.45
  118.8 3.2 %reduce = f32[8,20480]{1,0:T(8,128)} reduce(f32[8,1,20480]{2,1,0:T(1,128)S(1)} %all-to-all-done, f32[]{:T(128)} %broadcast.45), dimensions={1}, to_apply=%all_to_all.26.reduce_sub_computation | reduce | bytes 1310724 | tf_op jit(solution)/shard_map/all_to_all | solution.py:59
  121.9 3.1 %reshape.42 = f32[512,5,64]{2,1,0:T(8,128)} reshape(f32[8,20480]{1,0:T(8,128)} %reduce) | data formatting | bytes 1310720
  125.0 2.4 %copy.72 = f32[5,64,8,64]{1,2,3,0:T(8,128)S(1)} copy(f32[5,64,8,64]{1,0,3,2:T(8,128)} %bitcast.77) | data formatting | bytes 1310720 | tf_op jit(solution)/shard_map/all_to_all | solution.py:59
  127.4 0.0 copy-start.1
  127.4 1.1 copy-done.1
  128.4 0.7 slice_negate_fusion
  129.2 1.6 all_to_all.29
  130.8 1.1 neg.15
  131.9 2.3 %fusion = f32[5,64,1024]{2,1,0:T(8,128)S(1)} fusion(f32[5,512,64]{1,2,0:T(8,128)S(1)} %all_to_all.29, f32[512,1024]{1,0:T(8,128)S(1)} %copy-done), kind=kOutput, calls=%fused_computation | convolution fusion | flops 2013265920 | bytes 4063232 | tf_op jit(solution)/shard_map/vyx,yk->vxk/dot_general | solution.py:61
  134.2 0.2 fusion.9
  134.4 2.0 %copy.54 = f32[5,64,512]{1,0,2:T(8,128)} copy(f32[5,64,512]{2,1,0:T(8,128)S(1)} %fusion.9) | data formatting | bytes 1310720 | tf_op jit(solution)/shard_map/add | solution.py:63
  136.4 3.1 %reshape.43 = f32[8,1,20480]{2,1,0:T(1,128)} reshape(f32[512,5,64]{2,1,0:T(8,128)} %bitcast.78) | data formatting | bytes 1310720
  139.5 29.1 %all-to-all-start.1 = ((f32[8,1,20480]{2,1,0:T(1,128)}), f32[8,1,20480]{2,1,0:T(1,128)S(1)}, u32[]{:S(2)}, u32[]{:S(2)}) async-start(f32[8,1,20480]{2,1,0:T(1,128)} %reshape.43), calls=%async_computation.1 | async-start | bytes 1310720 | tf_op jit(solution)/shard_map/all_to_all | solution.py:64
  168.5 1.8 fusion.19
  170.3 5.3 %fusion.6 = f32[5,64,1024]{2,1,0:T(8,128)} fusion(f32[5,64,1024]{2,1,0:T(8,128)} %fusion.20, f32[5,64,512]{2,1,0:T(8,128)S(1)} %bitcast_multiply_fusion, f32[512,1024]{1,0:T(8,128)} %param.15), kind=kOutput, calls=%fused_computation.6 | convolution fusion | flops 2013593600 | bytes 5373952 | tf_op jit(solution)/shard_map/vyx,xk->vyk/dot_general | solution.py:56
  175.7 3.8 %all-to-all-done.1 = f32[8,1,20480]{2,1,0:T(1,128)S(1)} async-done(((f32[8,1,20480]{2,1,0:T(1,128)}), f32[8,1,20480]{2,1,0:T(1,128)S(1)}, u32[]{:S(2)}, u32[]{:S(2)}) %all-to-all-start.1) | async-done | bytes 655392 | tf_op jit(solution)/shard_map/all_to_all | solution.py:64
  179.4 2.1 %reduce.1 = f32[8,20480]{1,0:T(8,128)S(1)} reduce(f32[8,1,20480]{2,1,0:T(1,128)S(1)} %all-to-all-done.1, f32[]{:T(128)} %broadcast.45), dimensions={1}, to_apply=%all_to_all.30.reduce_sub_computation | reduce | bytes 1310724 | tf_op jit(solution)/shard_map/all_to_all | solution.py:64
  181.5 2.0 %reshape.44 = f32[512,5,64]{2,1,0:T(8,128)} reshape(f32[8,20480]{1,0:T(8,128)S(1)} %reduce.1) | data formatting | bytes 1310720
  183.5 2.4 %copy.71 = f32[5,64,8,64]{1,2,3,0:T(8,128)S(1)} copy(f32[5,64,8,64]{1,0,3,2:T(8,128)} %bitcast.79) | data formatting | bytes 1310720 | tf_op jit(solution)/shard_map/all_to_all | solution.py:64
  185.9 1.2 all_to_all.33
  187.0 2.9 %fusion.16 = f32[1,5,64,512]{3,2,1,0:T(8,128)} fusion(f32[5,64,1024]{2,1,0:T(8,128)} %fusion.6, f32[5,512,64]{1,2,0:T(8,128)} %all_to_all.33, f32[64,512]{1,0:T(8,128)} %get-tuple-element.8, f32[5]{0:T(128)S(1)} %compare_convert_fusion, f32[5]{0:T(128)S(1)} %bitcast.88, f32[64,512]{1,0:T(8,128)S(1)} %get-tuple-element.7, f32[64]{0:T(128)S(1)} %compare_convert_fusion.1, ...), kind=kLoop, calls=%fused_computation.19 | loop fusion | flops 1638400 | bytes 3539240 | tf_op jit(solution)/shard_map/broadcast_in_dim | solution.py:70
  (15 shorter events, 0.1 us)
Async XLA Ops:
  0.0 131.9 %copy-start = (f32[512,1024]{1,0:T(8,128)S(1)}, f32[512,1024]{1,0:T(8,128)}, u32[]{:S(2)}) copy-start(f32[512,1024]{1,0:T(8,128)} %param.17) | copy-start | bytes 6291460
  7.2 22.1 %copy-start.4 = (s32[128,2]{0,1:T(2,128)S(1)}, s32[128,2]{0,1:T(2,128)}, u32[]{:S(2)}) copy-start(s32[128,2]{0,1:T(2,128)} %param.12) | copy-start | bytes 3076
  7.2 22.1 %copy-start.5 = (s32[128,2]{0,1:T(2,128)S(1)}, s32[128,2]{0,1:T(2,128)}, u32[]{:S(2)}) copy-start(s32[128,2]{0,1:T(2,128)} %param.13) | copy-start | bytes 3076
  7.2 22.3 %copy-start.7 = (s32[128]{0:T(128)S(1)}, s32[128]{0:T(128)}, u32[]{:S(2)}) copy-start(s32[128]{0:T(128)} %param.11) | copy-start | bytes 1540
  7.2 24.9 %copy-start.3 = (f32[7]{0:T(128)S(1)}, f32[7]{0:T(128)}, u32[]{:S(2)}) copy-start(f32[7]{0:T(128)} %param.18) | copy-start | bytes 88
  10.3 108.0 %all-to-all-start = ((f32[8,1,20480]{2,1,0:T(1,128)}), f32[8,1,20480]{2,1,0:T(1,128)S(1)}, u32[]{:S(2)}, u32[]{:S(2)}) async-start(f32[8,1,20480]{2,1,0:T(1,128)} %reshape.41), calls=%async_computation | async-start | bytes 1310720 | tf_op jit(solution)/shard_map/all_to_all | solution.py:59
  34.8 81.1 %copy-start.6 = (f32[5]{0:T(128)S(1)}, f32[5]{0:T(128)}, u32[]{:S(2)}) copy-start(f32[5]{0:T(128)} %constant.28.clone) | copy-start | bytes 64
  34.8 81.2 %copy-start.2 = (f32[6,1024]{1,0:T(8,128)S(1)}, f32[6,1024]{1,0:T(8,128)}, u32[]{:S(2)}) copy-start(f32[6,1024]{1,0:T(8,128)} %param.16) | copy-start | bytes 73732
  127.4 1.1 copy-start.1
  139.5 39.9 %all-to-all-start.1 = ((f32[8,1,20480]{2,1,0:T(1,128)}), f32[8,1,20480]{2,1,0:T(1,128)S(1)}, u32[]{:S(2)}, u32[]{:S(2)}) async-start(f32[8,1,20480]{2,1,0:T(1,128)} %reshape.43), calls=%async_computation.1 | async-start | bytes 1310720 | tf_op jit(solution)/shard_map/all_to_all | solution.py:64
where the time goes:
time: 191 us; the launch traced here: 190 us
  blocking collectives  80.2 us (42%)
  starting transfers between devices  46.7 us (24%)
  local copies, waits for them, and re-layouts  29.3 us (15%)
  other arithmetic  17.2 us (9%)
  matrix products  10.7 us (6%)
  waiting for transfers between devices  3.75 us (2%)
  between operations  2.05 us (1%)
    all_gather x1, blocking collectives, on_device(): shard_piece = lax.all_gather(face_planes, 'blk', axis=0, tiled=True)  80.2 us
    all_to_all x1, starting transfers between devices, on_device(): lax.all_to_all(y_cols_term, 'line', split_axis=2, concat_axis=1, tiled=True)  29.1 us
    all_to_all x1, starting transfers between devices, on_device(): lax.all_to_all(masked, 'line', split_axis=2, concat_axis=1, tiled=True)  17.6 us
    unnamed x21, local copies, waits for them, and re-layouts  12.3 us
    dot_general x1, matrix products, on_device(): x_parts = jnp.einsum('vyx,xk->vyk', masked, x_operator, precision=highest)  5.32 us
    all_to_all x3, local copies, waits for them, and re-layouts, on_device(): lax.all_to_all(masked, 'line', split_axis=2, concat_axis=1, tiled=True)  4.47 us
  transfers between devices with their start and end apart: 2, of which 1 were waited for; matrix products, arithmetic and copies ran while one was open for 8% of the time, Pallas kernels for 0%

commit v1 on v0

v1 whole, which is shorter than its diff:
```python
import functools

import jax
import jax.numpy as jnp
from jax import lax
from jax.experimental import pallas as pl
from jax.experimental.pallas import tpu as pltpu
from jax.sharding import PartitionSpec as P

NY = 8
STEP = 0.3
MESH = pl.DeviceIdType.MESH
F32 = jnp.float32
BF16 = jnp.bfloat16
PEERS = ((1, 0), (3, 0), (1, 1), (3, 1), (2, 0), (2, 1), (0, 1))


def split(value):
    high = value.astype(BF16)
    return high, (value - high.astype(F32)).astype(BF16)


def mm(a, b):
    return jnp.dot(a, b, preferred_element_type=F32)


def kernel(
    nz,
    ny,
    flow,
    owner_h,
    link_block_h,
    link_side_h,
    rows_live_h,
    xop_h,
    gop_h,
    yop_h,
    coef_h,
    out,
    m,
    owner_v,
    link_block_v,
    link_side_v,
    rows_live_v,
    coef,
    gop,
    xop,
    yop,
    xh,
    xl,
    yth,
    ytl,
    mh,
    ml,
    s_ab,
    s_c,
    r_ab,
    r_c,
    t_ab,
    t_c,
    b_ab,
    b_c,
    vv,
    qcat,
    res,
    res2,
    acc,
    face,
    gz,
    sy,
    ry,
    load_sem,
    fs,
    fr,
    bs,
    br,
    zs,
    zr,
    ys,
    yr,
):
    line = lax.axis_index("line")
    slot = lax.axis_index("blk")
    chip, core = line // 2, lax.rem(line, 2)
    z, y = slot // ny, lax.rem(slot, ny)

    def peer(ahead, other):
        return lax.rem(chip + ahead, 4) * 2 + lax.rem(core + other, 2)

    def z_peer(d):
        return lax.rem(z + d, nz) * ny + y

    def y_peer(d):
        return z * ny + lax.rem(y + d, ny)

    barrier = pltpu.get_barrier_semaphore()
    for ahead, other in PEERS:
        pl.semaphore_signal(barrier, inc=1, device_id={"line": peer(ahead, other)}, device_id_type=MESH)

    @pl.loop(1, nz)
    def _(d):
        pl.semaphore_signal(barrier, inc=1, device_id={"blk": z_peer(d)}, device_id_type=MESH)

    @pl.loop(1, ny)
    def _(d):
        pl.semaphore_signal(barrier, inc=1, device_id={"blk": y_peer(d)}, device_id_type=MESH)

    loads = [
        pltpu.make_async_copy(a, b, load_sem.at[i])
        for i, (a, b) in enumerate(
            (
                (rows_live_h, rows_live_v),
                (owner_h, owner_v),
                (flow, m),
                (link_block_h, link_block_v),
                (link_side_h, link_side_v),
                (coef_h, coef),
                (gop_h, gop),
                (yop_h, yop),
                (xop_h, xop),
            )
        )
    ]
    for load in loads:
        load.start()
    loads[0].wait()
    loads[1].wait()

    lanes = lax.broadcasted_iota(jnp.int32, (64, 128), 1)
    lo = lanes < 64
    mine = owner_v[...] == slot
    live_rows = jnp.sum(jnp.where(mine, rows_live_v[...].astype(F32), 0.0), axis=1, keepdims=True)
    row_id = (lax.broadcasted_iota(jnp.int32, (64, 128), 0) + line * 64).astype(F32)
    live = (row_id < live_rows).astype(F32)
    loads[2].wait()

    for pair, (first, second) in enumerate(((1, 0), (2, 3))):
        for c in range(4):
            cols = slice(128 * c, 128 * c + 128)
            a = m[first, :, cols] * live
            b = m[second, :, cols] * live
            m[first, :, cols] = a
            m[second, :, cols] = b
            s_ab[pair, 2 * c] = jnp.where(lo, a, pltpu.roll(b, 64, 1))
            s_ab[pair, 2 * c + 1] = jnp.where(lo, pltpu.roll(a, 64, 1), b)
    lo32 = lo[:32]
    for c in range(4):
        cols = slice(128 * c, 128 * c + 128)
        a = m[4, :, cols] * live
        m[4, :, cols] = a
        s_c[2 * c] = jnp.where(lo32, a[:32], pltpu.roll(a[32:], 64, 1))
        s_c[2 * c + 1] = jnp.where(lo32, pltpu.roll(a[:32], 64, 1), a[32:])

    planes = []
    for v in range(5):
        planes.append(jnp.where(lanes < 3, m[v, :, 0:128], pltpu.roll(m[v, :, 384:512], 6, 1)))
    planes.append(jnp.zeros((64, 128), F32))
    for j in range(3):
        both = jnp.concatenate([planes[2 * j], planes[2 * j + 1]], axis=0)
        face[:, 128 * j : 128 * j + 128] = jnp.transpose(both)[:8]

    pl.semaphore_wait(barrier, len(PEERS) + nz - 1 + ny - 1)

    here = pl.ds(pl.multiple_of(line * 64, 64), 64)

    def forward(chunk, i):
        ahead, other = PEERS[i]
        to = peer(ahead, other)
        if chunk < 2:
            source, target = s_ab.at[chunk, to], r_ab.at[chunk, here]
        else:
            source, target = s_c.at[to], r_c.at[line]
        return pltpu.make_async_remote_copy(
            src_ref=source,
            dst_ref=target,
            send_sem=fs.at[chunk, i],
            recv_sem=fr.at[chunk, i],
            device_id={"line": to},
            device_id_type=MESH,
        )

    def backward(chunk, i):
        ahead, other = PEERS[i]
        to = peer(ahead, other)
        if chunk < 2:
            source = t_ab.at[chunk, pl.ds(pl.multiple_of(to * 64, 64), 64)]
            target = b_ab.at[chunk, line]
        else:
            source, target = t_c.at[to], b_c.at[line]
        return pltpu.make_async_remote_copy(
            src_ref=source,
            dst_ref=target,
            send_sem=bs.at[chunk, i],
            recv_sem=br.at[chunk, i],
            device_id={"line": to},
            device_id_type=MESH,
        )

    def z_copy(d):
        return pltpu.make_async_remote_copy(
            src_ref=face,
            dst_ref=gz.at[z],
            send_sem=zs.at[d],
            recv_sem=zr.at[d],
            device_id={"blk": z_peer(d)},
            device_id_type=MESH,
        )

    def y_copy(d):
        return pltpu.make_async_remote_copy(
            src_ref=sy.at[lax.rem(y + d, ny)],
            dst_ref=ry.at[y],
            send_sem=ys.at[d],
            recv_sem=yr.at[d],
            device_id={"blk": y_peer(d)},
            device_id_type=MESH,
        )

    for i in range(7):
        forward(0, i).start()

    @pl.loop(1, nz)
    def _(d):
        z_copy(d).start()

    for chunk in (1, 2):
        for i in range(7):
            forward(chunk, i).start()
    gz[z] = face[...]
    r_ab[0, here] = s_ab[0, line]
    r_ab[1, here] = s_ab[1, line]
    r_c[line] = s_c[line]

    loads[7].wait()

    @pl.loop(0, 8)
    def _(i):
        rows = pl.ds(pl.multiple_of(i * 128, 128), 128)
        for j in range(4):
            block = jnp.transpose(yop[128 * j : 128 * j + 128, rows])
            high, low = split(block)
            yth[rows, 128 * j : 128 * j + 128] = high
            ytl[rows, 128 * j : 128 * j + 128] = low

    loads[3].wait()
    loads[4].wait()
    peers_row = lax.broadcasted_iota(jnp.int32, (ny, nz * ny), 0) + z * ny
    lane_row = lax.broadcasted_iota(jnp.int32, (ny, nz * ny), 1).astype(F32)
    owner = owner_v[...]
    owner_f = owner.astype(F32)
    hot = owner == peers_row
    wanted = []
    for side in range(2):
        partner = jnp.sum(
            jnp.where(hot, link_block_v[side : side + 1, :].astype(F32), 0.0), axis=1, keepdims=True
        )
        far = jnp.sum(
            jnp.where(hot, link_side_v[side : side + 1, :].astype(F32), 0.0), axis=1, keepdims=True
        )
        source = jnp.sum(jnp.where(lane_row == partner, owner_f, 0.0), axis=1, keepdims=True)
        wanted.append((source, far))

    @pl.loop(1, nz)
    def _(d):
        z_copy(d).wait_recv()

    plane_row = lax.broadcasted_iota(jnp.int32, (8, 384), 0)
    for p in range(ny):
        parts = []
        for side in range(2):
            source = jnp.broadcast_to(wanted[side][0][p : p + 1], (8, 384))
            far = jnp.broadcast_to(wanted[side][1][p : p + 1], (8, 384))
            total = jnp.zeros((8, 384), F32)
            for zz in range(nz):
                code = (y + zz * ny).astype(F32)
                total = total + jnp.where(source == code, gz[zz], 0.0)
            parts.append(jnp.where(far < 0.5, total, pltpu.roll(total, 5, 0)))
        sy[p] = jnp.where(plane_row < 3, parts[0], pltpu.roll(parts[1], 3, 0))

    @pl.loop(1, ny)
    def _(d):
        y_copy(d).start()

    ry[y] = sy[y]

    loads[5].wait()
    nu = [coef[v] for v in range(5)]

    def y_pair(pair, nu_first, nu_second):
        nu_lane = STEP * jnp.where(lo, nu_first, nu_second)
        high, low = split(r_ab[pair])
        qcat[:, :128] = high
        qcat[:, 128:] = low
        res[...] = mm(yth[...], qcat[...])
        res2[...] = mm(ytl[...], qcat[:, :128])

        @pl.loop(0, 8)
        def _(i):
            a = pl.ds(pl.multiple_of(i * 64, 64), 64)
            b = pl.ds(pl.multiple_of(i * 64 + 512, 64), 64)
            dy = res[a, :128] + res[a, 128:] + res2[a]
            dyy = res[b, :128] + res[b, 128:] + res2[b]
            t_ab[pair, a] = nu_lane * dyy - vv[a] * dy

    for i in range(7):
        forward(0, i).wait_recv()
    first = r_ab[0]
    lo_all = lax.broadcasted_iota(jnp.int32, (512, 128), 1) < 64
    vv[...] = STEP * jnp.where(lo_all, first, pltpu.roll(first, 64, 1))
    y_pair(0, nu[1], nu[0])
    for i in range(7):
        backward(0, i).start()
    b_ab[0, line] = t_ab[0, here]

    for i in range(7):
        forward(1, i).wait_recv()
    y_pair(1, nu[2], nu[3])
    for i in range(7):
        backward(1, i).start()
    b_ab[1, line] = t_ab[1, here]

    for i in range(7):
        forward(2, i).wait_recv()
    for s in range(8):
        part = r_c[s]
        turned = pltpu.roll(part, 64, 1)
        for half, (keep, other) in enumerate(((part, turned), (turned, part))):
            high = keep.astype(BF16).astype(F32)
            low = other - other.astype(BF16).astype(F32)
            rows = slice(64 * s + 32 * half, 64 * s + 32 * half + 32)
            qcat[rows, :128] = jnp.where(lo32, high, low).astype(BF16)
    res2[...] = mm(yth[...], qcat[:, :128]) + mm(ytl[...], qcat[:, :128])

    @pl.loop(0, 8)
    def _(i):
        a = pl.ds(pl.multiple_of(i * 64, 64), 64)
        b = pl.ds(pl.multiple_of(i * 64 + 512, 64), 64)
        dy = res2[a] + pltpu.roll(res2[a], 64, 1)
        dyy = res2[b] + pltpu.roll(res2[b], 64, 1)
        term = (STEP * nu[4]) * dyy - vv[a] * dy
        t_c[i] = jnp.where(lo32, term[:32], term[32:])

    for i in range(7):
        backward(2, i).start()
    b_c[line] = t_c[line]

    own = []
    for side in range(2):
        own.append(
            jnp.sum(jnp.where(mine, link_side_v[side : side + 1, :].astype(F32), 0.0), axis=1, keepdims=True)
        )

    @pl.loop(1, ny)
    def _(d):
        y_copy(d).wait_recv()

    ghost = ry[0]
    for p in range(1, ny):
        ghost = ghost + ry[p]
    flip = jnp.where(plane_row < 3, 1.0 - own[0], own[1])
    turned = jnp.where(
        (plane_row == 0) | (plane_row == 3),
        pltpu.roll(ghost, 6, 0),
        jnp.where((plane_row == 2) | (plane_row == 5), pltpu.roll(ghost, 2, 0), ghost),
    )
    column = lax.broadcasted_iota(jnp.int32, (8, 384), 1)
    turned = jnp.where(column < 64, -turned, turned)
    ghost = jnp.where(flip > 0.5, turned, ghost)
    ghost = jnp.where(plane_row < 6, ghost, 0.0)
    ghost_high = ghost.astype(BF16).astype(F32)
    stack = jnp.concatenate([ghost_high, ghost - ghost_high, ghost_high, jnp.zeros((104, 384), F32)], axis=0)
    ghost_t = jnp.concatenate(
        [jnp.transpose(stack[:, 128 * j : 128 * j + 128]) for j in range(3)], axis=0
    )[:320].astype(BF16)
    loads[6].wait()
    g_op = jnp.concatenate([gop[...], jnp.zeros((2, 1024), F32)], axis=0)
    g_high = g_op.astype(BF16).astype(F32)
    g_stack = jnp.concatenate(
        [g_high, g_high, g_op - g_high, jnp.zeros((104, 1024), F32)], axis=0
    ).astype(BF16)
    gop_stack = g_stack

    loads[8].wait()

    @pl.loop(0, 8)
    def _(i):
        rows = pl.ds(pl.multiple_of(i * 64, 64), 64)
        high, low = split(xop[rows])
        xh[rows] = high
        xl[rows] = low

    for v in range(5):
        high, low = split(m[v])
        mh[64 * v : 64 * v + 64] = high
        ml[64 * v : 64 * v + 64] = low
    for n in range(2):
        deriv = []
        for o in range(2):
            cols = slice(512 * o + 256 * n, 512 * o + 256 * n + 256)
            deriv.append(
                mm(mh[...], xh[:, cols])
                + mm(ml[...], xh[:, cols])
                + mm(mh[...], xl[:, cols])
                + mm(ghost_t, gop_stack[:, cols])
            )
        cols = slice(256 * n, 256 * n + 256)
        u = STEP * m[0, :, cols]
        for v in range(5):
            rows = slice(64 * v, 64 * v + 64)
            term = m[v, :, cols] + (STEP * nu[v]) * deriv[1][rows] - u * deriv[0][rows]
            if v == 1:
                term = term + (STEP * coef[5]) * m[3, :, cols] + (STEP * coef[6]) * m[4, :, cols]
            acc[v, :, cols] = term

    for pair, (one, two) in enumerate(((1, 0), (2, 3))):
        for i in range(7):
            backward(pair, i).wait_recv()
        for c in range(4):
            cols = slice(128 * c, 128 * c + 128)
            a, b = b_ab[pair, 2 * c], b_ab[pair, 2 * c + 1]
            out[one, :, cols] = live * (acc[one, :, cols] + jnp.where(lo, a, pltpu.roll(b, 64, 1)))
            out[two, :, cols] = live * (acc[two, :, cols] + jnp.where(lo, pltpu.roll(a, 64, 1), b))
    for i in range(7):
        backward(2, i).wait_recv()
    for c in range(4):
        cols = slice(128 * c, 128 * c + 128)
        a, b = b_c[2 * c], b_c[2 * c + 1]
        top = jnp.where(lo32, a, pltpu.roll(b, 64, 1))
        bottom = jnp.where(lo32, pltpu.roll(a, 64, 1), b)
        out[4, :32, cols] = live[:32] * (acc[4, :32, cols] + top)
        out[4, 32:, cols] = live[32:] * (acc[4, 32:, cols] + bottom)

    for chunk in range(3):
        for i in range(7):
            forward(chunk, i).wait_send()
            backward(chunk, i).wait_send()

    @pl.loop(1, nz)
    def _(d):
        z_copy(d).wait_send()

    @pl.loop(1, ny)
    def _(d):
        y_copy(d).wait_send()


def on_device(
    nz,
    ny,
    flow_state,
    block_owner,
    link_block,
    link_side,
    rows_live,
    x_operator,
    ghost_operator,
    y_operator,
    coefficients,
):
    any_spec = pl.BlockSpec(memory_space=pltpu.HBM)
    dma = pltpu.SemaphoreType.DMA
    blocks = nz * ny
    result = pl.pallas_call(
        functools.partial(kernel, nz, ny),
        out_shape=jax.ShapeDtypeStruct((5, 64, 512), F32),
        in_specs=[any_spec] * 9,
        out_specs=pl.BlockSpec(memory_space=pltpu.VMEM),
        scratch_shapes=[
            pltpu.VMEM((5, 64, 512), F32),
            pltpu.VMEM((1, blocks), jnp.int32),
            pltpu.VMEM((2, blocks), jnp.int32),
            pltpu.VMEM((2, blocks), jnp.int32),
            pltpu.VMEM((1, blocks), jnp.int32),
            pltpu.SMEM((7,), F32),
            pltpu.VMEM((6, 1024), F32),
            pltpu.VMEM((512, 1024), F32),
            pltpu.VMEM((512, 1024), F32),
            pltpu.VMEM((512, 1024), BF16),
            pltpu.VMEM((512, 1024), BF16),
            pltpu.VMEM((1024, 512), BF16),
            pltpu.VMEM((1024, 512), BF16),
            pltpu.VMEM((320, 512), BF16),
            pltpu.VMEM((320, 512), BF16),
            pltpu.VMEM((2, 8, 64, 128), F32),
            pltpu.VMEM((8, 32, 128), F32),
            pltpu.VMEM((2, 512, 128), F32),
            pltpu.VMEM((8, 32, 128), F32),
            pltpu.VMEM((2, 512, 128), F32),
            pltpu.VMEM((8, 32, 128), F32),
            pltpu.VMEM((2, 8, 64, 128), F32),
            pltpu.VMEM((8, 32, 128), F32),
            pltpu.VMEM((512, 128), F32),
            pltpu.VMEM((512, 256), BF16),
            pltpu.VMEM((1024, 256), F32),
            pltpu.VMEM((1024, 128), F32),
            pltpu.VMEM((5, 64, 512), F32),
            pltpu.VMEM((8, 384), F32),
            pltpu.VMEM((nz, 8, 384), F32),
            pltpu.VMEM((ny, 8, 384), F32),
            pltpu.VMEM((ny, 8, 384), F32),
            dma((9,)),
            dma((3, 7)),
            dma((3, 7)),
            dma((3, 7)),
            dma((3, 7)),
            dma((nz,)),
            dma((nz,)),
            dma((ny,)),
            dma((ny,)),
        ],
        compiler_params=pltpu.CompilerParams(
            collective_id=0, has_side_effects=True, vmem_limit_bytes=56 * 1024 * 1024
        ),
        cost_estimate=pl.CostEstimate(flops=2 * 10**9, bytes_accessed=6 * 10**6, transcendentals=0),
    )(
        flow_state[0],
        block_owner[None],
        link_block.T,
        link_side.T,
        rows_live[None],
        x_operator,
        ghost_operator,
        y_operator,
        coefficients,
    )
    return result[None]


def solution(mesh):
    blocks = mesh.shape["blk"]
    ny = min(NY, blocks // 2)
    return jax.shard_map(
        functools.partial(on_device, blocks // ny, ny),
        mesh=mesh,
        in_specs=(P("blk", None, "line", None), P(), P(), P(), P(), P(), P(), P(), P()),
        out_specs=P("blk", None, "line", None),
        check_vma=False,
    )
```

time: 191 us -> 48.3 us (0.25)
  blocking collectives: 80.2 us -> 0 us
  starting transfers between devices: 46.7 us -> 0 us
  Pallas kernels: 0 us -> 46.1 us
  local copies, waits for them, and re-layouts: 29.3 us -> 1.99 us
  other arithmetic: 17.2 us -> 0 us
  matrix products: 10.7 us -> 0 us
  waiting for transfers between devices: 3.75 us -> 0 us
  between operations: 2.05 us -> 0.01 us
    all_gather x1 -> x0, blocking collectives: 80.2 us -> none  [on_device(): shard_piece = lax.all_gather(face_planes, 'blk', axis=0, tiled=True)]
    all_to_all x2 -> x0, starting transfers between devices: 46.7 us -> none  [the longest x1 29.1 us: on_device(): lax.all_to_all(y_cols_term, 'line', split_axis=2, concat_axis=1, tiled=True)]
    pallas_call x0 -> x1, Pallas kernels: none -> 46.1 us  [on_device(): pl.pallas_call(functools.partial(kernel, nz, ny), out_shape=jax.ShapeDtyp...]
    dot_general x4 -> x0, matrix products: 10.7 us -> none  [the longest x1 5.32 us: on_device(): x_parts = jnp.einsum('vyx,xk->vyk', masked, x_operator, precision=highest)]
    unnamed x21 -> x1, local copies, waits for them, and re-layouts: 12.3 us -> 1.99 us
    all_to_all x5 -> x0, local copies, waits for them, and re-layouts: 7.99 us -> none  [the longest x3 4.47 us: on_device(): lax.all_to_all(masked, 'line', split_axis=2, concat_axis=1, tiled=True)]
    all_to_all x2 -> x0, other arithmetic: 5.25 us -> none  [the longest x1 3.15 us: on_device(): lax.all_to_all(masked, 'line', split_axis=2, concat_axis=1, tiled=True)]
    all_to_all x2 -> x0, waiting for transfers between devices: 3.75 us -> none  [the longest x1 3.75 us: on_device(): lax.all_to_all(y_cols_term, 'line', split_axis=2, concat_axis=1, tiled=True)]
  transfers between devices with their start and end apart: 2 -> 0, of which waited for: 1 -> 0; matrix products, arithmetic and copies ran while one was open for 8% -> 0% of each run, Pallas kernels for 0% -> 0%
where the time goes in v1:
time: 48.3 us; the launch traced here: 48.1 us
  Pallas kernels  46.1 us (95%)
  local copies, waits for them, and re-layouts  1.99 us (4%)
    pallas_call x1, Pallas kernels, on_device(): pl.pallas_call(functools.partial(kernel, nz, ny), out_shape=jax.ShapeDtyp...  46.1 us
    unnamed x1, local copies, waits for them, and re-layouts  1.99 us

profile of v1, /device:TPU:1, one launch (start us, length us, event | category | flops | bytes accessed | tf_op | source)
XLA Modules:
  0.0 48.1 jit_solution(5608348501563480360)
XLA Ops:
  0.0 46.1 %shard_map.91 = f32[5,64,512]{2,1,0:T(8,128)} custom-call(f32[5,64,512]{2,1,0:T(8,128)} %bitcast.7, s32[1,128]{1,0:T(1,128)} %bitcast.10, s32[2,128]{1,0:T(2,128)} %bitcast.8, s32[2,128]{1,0:T(2,128)} %bitcast.9, s32[1,128]{1,0:T(1,128)} %bitcast.11, f32[512,1024]{1,0:T(8,128)} %xop_h.1, f32[6,1024]{1,0:T(8,128)} %gop_h.1, f32[512,1024]{1,0:T(8,128)} %yop_h.1, ...), custom_call_target="tpu_custom_call" | custom-call | flops 2000000000 | bytes 6000000 | tf_op jit(solution)/shard_map/pallas_call | solution.py:463
  46.1 2.0 %copy.11 = f32[1,5,64,512]{3,2,1,0:T(8,128)} copy(f32[1,5,64,512]{3,2,1,0:T(8,128)} %bitcast.6) | data formatting | bytes 1310720

commit v2 on v1

--- a/solution.py
+++ b/solution.py
@@ -27,6 +27,7 @@
 def kernel(
     nz,
     ny,
+    z_late,
     flow,
     owner_h,
     link_block_h,
@@ -78,6 +79,8 @@
     zr,
     ys,
     yr,
+    ready,
+    gstack,
 ):
     line = lax.axis_index("line")
     slot = lax.axis_index("blk")
@@ -87,23 +90,52 @@
     def peer(ahead, other):
         return lax.rem(chip + ahead, 4) * 2 + lax.rem(core + other, 2)
 
-    def z_peer(d):
-        return lax.rem(z + d, nz) * ny + y
-
-    def y_peer(d):
-        return z * ny + lax.rem(y + d, ny)
+    is_first = (slot == 0) & (line == 0)
+    late_line = (slot == 0) & (line != 0)
+    z_special = (y == 0) & (line == 0)
+    y_special = (z == 0) & (line == 0) & (y != 0)
+
+    def z_start(zz):
+        usual = jnp.where(zz < 8, 15 * zz, 88 + 4 * zz)
+        return jnp.where(z_special & (zz == 0), z_late, usual)
+
+    my_z = z_start(z)
+
+    def z_close(zz):
+        near = jnp.abs(z_start(zz) - my_z) <= 10
+        return near & jnp.logical_not(z_special & ((zz == 0) | (z == 0)))
+
+    def z_now(zz):
+        return (zz != z) & ((z_start(zz) < my_z) | z_close(zz))
+
+    def z_after(zz, least, most):
+        gap = z_start(zz) - my_z
+        return (gap > least) & (gap <= most) & jnp.logical_not(z_close(zz))
 
     barrier = pltpu.get_barrier_semaphore()
-    for ahead, other in PEERS:
-        pl.semaphore_signal(barrier, inc=1, device_id={"line": peer(ahead, other)}, device_id_type=MESH)
-
-    @pl.loop(1, nz)
-    def _(d):
-        pl.semaphore_signal(barrier, inc=1, device_id={"blk": z_peer(d)}, device_id_type=MESH)
-
-    @pl.loop(1, ny)
-    def _(d):
-        pl.semaphore_signal(barrier, inc=1, device_id={"blk": y_peer(d)}, device_id_type=MESH)
+
+    @pl.when(jnp.logical_not(is_first))
+    def _():
+        for ahead, other in PEERS:
+            pl.semaphore_signal(
+                barrier, inc=1, device_id={"line": peer(ahead, other)}, device_id_type=MESH
+            )
+
+    waits = len(PEERS) - jnp.where(late_line, 1, 0) + ny - 1 - jnp.where(y_special, 1, 0)
+    for zz in range(nz):
+        waits += jnp.where(z_now(zz), 1, 0)
+
+    @pl.loop(0, nz)
+    def _(zz):
+        @pl.when((zz != z) & ((z_start(zz) > my_z) | z_close(zz)))
+        def _():
+            pl.semaphore_signal(barrier, inc=1, device_id={"blk": zz * ny + y}, device_id_type=MESH)
+
+    @pl.loop(0, ny)
+    def _(yy):
+        @pl.when((yy != y) & jnp.logical_not(is_first))
+        def _():
+            pl.semaphore_signal(barrier, inc=1, device_id={"blk": z * ny + yy}, device_id_type=MESH)
 
     loads = [
         pltpu.make_async_copy(a, b, load_sem.at[i])
@@ -123,6 +155,19 @@
     ]
     for load in loads:
         load.start()
+
+    @pl.when(is_first)
+    def _():
+        pl.semaphore_wait(barrier, waits)
+        for ahead, other in PEERS:
+            pl.semaphore_signal(
+                ready, inc=1, device_id={"line": peer(ahead, other)}, device_id_type=MESH
+            )
+
+        @pl.loop(1, ny)
+        def _(yy):
+            pl.semaphore_signal(ready, inc=1, device_id={"blk": z * ny + yy}, device_id_type=MESH)
+
     loads[0].wait()
     loads[1].wait()
 
@@ -154,12 +199,18 @@
     planes = []
     for v in range(5):
         planes.append(jnp.where(lanes < 3, m[v, :, 0:128], pltpu.roll(m[v, :, 384:512], 6, 1)))
-    planes.append(jnp.zeros((64, 128), F32))
-    for j in range(3):
+    last = planes[4]
+    for v, moves in enumerate(((6, 6), (3, 3), (4, None), (1, None))):
+        for lane, move in zip((6, 7), moves):
+            if move is not None:
+                planes[v] = jnp.where(lanes == lane, pltpu.roll(last, move, 1), planes[v])
+    for j in range(2):
         both = jnp.concatenate([planes[2 * j], planes[2 * j + 1]], axis=0)
         face[:, 128 * j : 128 * j + 128] = jnp.transpose(both)[:8]
 
-    pl.semaphore_wait(barrier, len(PEERS) + nz - 1 + ny - 1)
+    @pl.when(jnp.logical_not(is_first))
+    def _():
+        pl.semaphore_wait(barrier, waits)
 
     here = pl.ds(pl.multiple_of(line * 64, 64), 64)
 
@@ -196,36 +247,44 @@
             device_id_type=MESH,
         )
 
-    def z_copy(d):
+    def z_copy(zz, sender):
         return pltpu.make_async_remote_copy(
             src_ref=face,
-            dst_ref=gz.at[z],
-            send_sem=zs.at[d],
-            recv_sem=zr.at[d],
-            device_id={"blk": z_peer(d)},
+            dst_ref=gz.at[sender],
+            send_sem=zs.at[zz],
+            recv_sem=zr.at[sender],
+            device_id={"blk": zz * ny + y},
             device_id_type=MESH,
         )
 
-    def y_copy(d):
+    def y_copy(yy, sender):
         return pltpu.make_async_remote_copy(
-            src_ref=sy.at[lax.rem(y + d, ny)],
-            dst_ref=ry.at[y],
-            send_sem=ys.at[d],
-            recv_sem=yr.at[d],
-            device_id={"blk": y_peer(d)},
+            src_ref=sy.at[yy],
+            dst_ref=ry.at[sender],
+            send_sem=ys.at[yy],
+            recv_sem=yr.at[sender],
+            device_id={"blk": z * ny + yy},
             device_id_type=MESH,
         )
 
-    for i in range(7):
-        forward(0, i).start()
-
-    @pl.loop(1, nz)
-    def _(d):
-        z_copy(d).start()
-
-    for chunk in (1, 2):
+    def is_late(i):
+        return late_line & (peer(*PEERS[i]) == 0)
+
+    def send_forward(chunk, i):
+        @pl.when(jnp.logical_not(is_late(i)))
+        def _():
+            forward(chunk, i).start()
+
+    @pl.loop(0, nz)
+    def _(zz):
+        @pl.when(z_now(zz))
+        def _():
+            z_copy(zz, z).start()
+
+    for chunk in range(3):
         for i in range(7):
-            forward(chunk, i).start()
+            send_forward(chunk, i)
+
     gz[z] = face[...]
     r_ab[0, here] = s_ab[0, line]
     r_ab[1, here] = s_ab[1, line]
@@ -260,28 +319,85 @@
         source = jnp.sum(jnp.where(lane_row == partner, owner_f, 0.0), axis=1, keepdims=True)
         wanted.append((source, far))
 
-    @pl.loop(1, nz)
-    def _(d):
-        z_copy(d).wait_recv()
+    own = []
+    for side in range(2):
+        own.append(
+            jnp.sum(jnp.where(mine, link_side_v[side : side + 1, :].astype(F32), 0.0), axis=1, keepdims=True)
+        )
+
+    loads[6].wait()
+    g_op = jnp.concatenate([gop[...], jnp.zeros((2, 1024), F32)], axis=0)
+    g_high = g_op.astype(BF16).astype(F32)
+    gstack[...] = jnp.concatenate(
+        [g_high, g_high, g_op - g_high, jnp.zeros((104, 1024), F32)], axis=0
+    ).astype(BF16)
 
     plane_row = lax.broadcasted_iota(jnp.int32, (8, 384), 0)
-    for p in range(ny):
-        parts = []
-        for side in range(2):
-            source = jnp.broadcast_to(wanted[side][0][p : p + 1], (8, 384))
-            far = jnp.broadcast_to(wanted[side][1][p : p + 1], (8, 384))
-            total = jnp.zeros((8, 384), F32)
-            for zz in range(nz):
-                code = (y + zz * ny).astype(F32)
-                total = total + jnp.where(source == code, gz[zz], 0.0)
-            parts.append(jnp.where(far < 0.5, total, pltpu.roll(total, 5, 0)))
-        sy[p] = jnp.where(plane_row < 3, parts[0], pltpu.roll(parts[1], 3, 0))
-
-    @pl.loop(1, ny)
-    def _(d):
-        y_copy(d).start()
-
-    ry[y] = sy[y]
+    wide_row = plane_row[:, :256]
+    half = lax.rem(lax.broadcasted_iota(jnp.int32, (8, 256), 1), 128) // 64
+    of_face = [
+        ((wide_row >= 3 * f) & (wide_row < 3 * f + 3)) | ((wide_row >= 6) & (half == f))
+        for f in range(2)
+    ]
+
+    def answer(least, most):
+        @pl.loop(1, nz + 1)
+        def _(step):
+            zz = lax.rem(step, nz)
+
+            @pl.when(z_after(zz, least, most))
+            def _():
+                z_copy(zz, zz).wait_recv()
+                z_copy(zz, z).start()
+
+    def ghost_stage():
+        answer(60, 1000)
+
+        @pl.loop(0, nz)
+        def _(zz):
+            @pl.when(z_now(zz))
+            def _():
+                z_copy(zz, zz).wait_recv()
+
+        for p in range(ny):
+            message = jnp.zeros((8, 256), F32)
+            for side in range(2):
+                source = jnp.broadcast_to(wanted[side][0][p : p + 1], (8, 256))
+                far = jnp.broadcast_to(wanted[side][1][p : p + 1], (8, 256))
+                total = jnp.zeros((8, 256), F32)
+                for zz in range(nz):
+                    code = (y + zz * ny).astype(F32)
+                    total = total + jnp.where(source == code, gz[zz], 0.0)
+                halves = jnp.concatenate(
+                    [pltpu.roll(total[:, 128 * j : 128 * j + 128], 64, 1) for j in range(2)], axis=1
+                )
+                swapped = jnp.where(wide_row < 6, pltpu.roll(total, 3 if side else 5, 0), halves)
+                chosen = jnp.where(jnp.abs(far - side) < 0.5, total, swapped)
+                message = jnp.where(of_face[side], chosen, message)
+            sy[p] = message
+
+        @pl.when(y_special)
+        def _():
+            pl.semaphore_wait(ready, 1)
+
+        @pl.loop(0, ny)
+        def _(yy):
+            @pl.when(yy != y)
+            def _():
+                y_copy(yy, y).start()
+
+        ry[y] = sy[y]
+
+    @pl.when(late_line)
+    def _():
+        pl.semaphore_wait(ready, 1)
+
+    for chunk in range(3):
+        for i in range(7):
+
+            @pl.when(is_late(i))
+            def _():
+                forward(chunk, i).start()
 
     loads[5].wait()
     nu = [coef[v] for v in range(5)]
@@ -304,10 +420,11 @@
 
     for i in range(7):
         forward(0, i).wait_recv()
-    first = r_ab[0]
+    start = r_ab[0]
     lo_all = lax.broadcasted_iota(jnp.int32, (512, 128), 1) < 64
-    vv[...] = STEP * jnp.where(lo_all, first, pltpu.roll(first, 64, 1))
+    vv[...] = STEP * jnp.where(lo_all, start, pltpu.roll(start, 64, 1))
     y_pair(0, nu[1], nu[0])
+    answer(0, 30)
     for i in range(7):
         backward(0, i).start()
     b_ab[0, line] = t_ab[0, here]
@@ -315,6 +432,7 @@
     for i in range(7):
         forward(1, i).wait_recv()
     y_pair(1, nu[2], nu[3])
+    answer(30, 60)
     for i in range(7):
         backward(1, i).start()
     b_ab[1, line] = t_ab[1, here]
@@ -344,19 +462,63 @@
         backward(2, i).start()
     b_c[line] = t_c[line]
 
-    own = []
-    for side in range(2):
-        own.append(
-            jnp.sum(jnp.where(mine, link_side_v[side : side + 1, :].astype(F32), 0.0), axis=1, keepdims=True)
-        )
-
-    @pl.loop(1, ny)
-    def _(d):
-        y_copy(d).wait_recv()
+    loads[8].wait()
+
+    @pl.loop(0, 8)
+    def _(i):
+        rows = pl.ds(pl.multiple_of(i * 64, 64), 64)
+        high, low = split(xop[rows])
+        xh[rows] = high
+        xl[rows] = low
+
+    for v in range(5):
+        high, low = split(m[v])
+        mh[64 * v : 64 * v + 64] = high
+        ml[64 * v : 64 * v + 64] = low
+    for n in range(2):
+        deriv = []
+        for o in range(2):
+            cols = slice(512 * o + 256 * n, 512 * o + 256 * n + 256)
+            deriv.append(
+                mm(mh[...], xh[:, cols])
+                + mm(ml[...], xh[:, cols])
+                + mm(mh[...], xl[:, cols])
+            )
+        cols = slice(256 * n, 256 * n + 256)
+        u = STEP * m[0, :, cols]
+        for v in range(5):
+            rows = slice(64 * v, 64 * v + 64)
+            term = m[v, :, cols] + (STEP * nu[v]) * deriv[1][rows] - u * deriv[0][rows]
+            if v == 1:
+                term = term + (STEP * coef[5]) * m[3, :, cols] + (STEP * coef[6]) * m[4, :, cols]
+            acc[v, :, cols] = term
+
+    ghost_stage()
+
+    for pair, (first, second) in enumerate(((1, 0), (2, 3))):
+        for i in range(7):
+            backward(pair, i).wait_recv()
+        for c in range(4):
+            cols = slice(128 * c, 128 * c + 128)
+            a, b = b_ab[pair, 2 * c], b_ab[pair, 2 * c + 1]
+            acc[first, :, cols] += jnp.where(lo, a, pltpu.roll(b, 64, 1))
+            acc[second, :, cols] += jnp.where(lo, pltpu.roll(a, 64, 1), b)
+
+    @pl.loop(0, ny)
+    def _(yy):
+        @pl.when(yy != y)
+        def _():
+            y_copy(yy, yy).wait_recv()
 
     ghost = ry[0]
     for p in range(1, ny):
         ghost = ghost + ry[p]
+    one, two = ghost[:, :128], ghost[:, 128:]
+    row = plane_row[:, :128]
+    last = jnp.where(row < 2, pltpu.roll(one, 2, 0), pltpu.roll(two, 4, 0))
+    last = jnp.where((row == 3) | (row == 4), pltpu.roll(pltpu.roll(one, 64, 1), 5, 0), last)
+    last = jnp.where(row == 5, pltpu.roll(pltpu.roll(two, 64, 1), 7, 0), last)
+    ghost = jnp.concatenate([one, two, jnp.where(lanes[:8] < 64, last, 0.0)], axis=1)
     flip = jnp.where(plane_row < 3, 1.0 - own[0], own[1])
     turned = jnp.where(
         (plane_row == 0) | (plane_row == 3),
@@ -372,54 +534,19 @@
     ghost_t = jnp.concatenate(
         [jnp.transpose(stack[:, 128 * j : 128 * j + 128]) for j in range(3)], axis=0
     )[:320].astype(BF16)
-    loads[6].wait()
-    g_op = jnp.concatenate([gop[...], jnp.zeros((2, 1024), F32)], axis=0)
-    g_high = g_op.astype(BF16).astype(F32)
-    g_stack = jnp.concatenate(
-        [g_high, g_high, g_op - g_high, jnp.zeros((104, 1024), F32)], axis=0
-    ).astype(BF16)
-    gop_stack = g_stack
-
-    loads[8].wait()
-
-    @pl.loop(0, 8)
-    def _(i):
-        rows = pl.ds(pl.multiple_of(i * 64, 64), 64)
-        high, low = split(xop[rows])
-        xh[rows] = high
-        xl[rows] = low
-
-    for v in range(5):
-        high, low = split(m[v])
-        mh[64 * v : 64 * v + 64] = high
-        ml[64 * v : 64 * v + 64] = low
     for n in range(2):
-        deriv = []
-        for o in range(2):
-            cols = slice(512 * o + 256 * n, 512 * o + 256 * n + 256)
-            deriv.append(
-                mm(mh[...], xh[:, cols])
-                + mm(ml[...], xh[:, cols])
-                + mm(mh[...], xl[:, cols])
-                + mm(ghost_t, gop_stack[:, cols])
-            )
         cols = slice(256 * n, 256 * n + 256)
+        dx = mm(ghost_t, gstack[:, cols])
+        dxx = mm(ghost_t, gstack[:, 256 * n + 512 : 256 * n + 768])
         u = STEP * m[0, :, cols]
         for v in range(5):
             rows = slice(64 * v, 64 * v + 64)
-            term = m[v, :, cols] + (STEP * nu[v]) * deriv[1][rows] - u * deriv[0][rows]
-            if v == 1:
-                term = term + (STEP * coef[5]) * m[3, :, cols] + (STEP * coef[6]) * m[4, :, cols]
-            acc[v, :, cols] = term
-
-    for pair, (one, two) in enumerate(((1, 0), (2, 3))):
-        for i in range(7):
-            backward(pair, i).wait_recv()
-        for c in range(4):
-            cols = slice(128 * c, 128 * c + 128)
-            a, b = b_ab[pair, 2 * c], b_ab[pair, 2 * c + 1]
-            out[one, :, cols] = live * (acc[one, :, cols] + jnp.where(lo, a, pltpu.roll(b, 64, 1)))
-            out[two, :, cols] = live * (acc[two, :, cols] + jnp.where(lo, pltpu.roll(a, 64, 1), b))
+            term = acc[v, :, cols] + (STEP * nu[v]) * dxx[rows] - u * dx[rows]
+            if v < 4:
+                out[v, :, cols] = jnp.concatenate([live, live], axis=1) * term
+            else:
+                acc[v, :, cols] = term
+
     for i in range(7):
         backward(2, i).wait_recv()
     for c in range(4):
@@ -435,13 +562,17 @@
             forward(chunk, i).wait_send()
             backward(chunk, i).wait_send()
 
-    @pl.loop(1, nz)
-    def _(d):
-        z_copy(d).wait_send()
-
-    @pl.loop(1, ny)
-    def _(d):
-        y_copy(d).wait_send()
+    @pl.loop(0, nz)
+    def _(zz):
+        @pl.when(zz != z)
+        def _():
+            z_copy(zz, z).wait_send()
+
+    @pl.loop(0, ny)
+    def _(yy):
+        @pl.when(yy != y)
+        def _():
+            y_copy(yy, y).wait_send()
 
 
 def on_device(
@@ -461,7 +592,7 @@
     dma = pltpu.SemaphoreType.DMA
     blocks = nz * ny
     result = pl.pallas_call(
-        functools.partial(kernel, nz, ny),
+        functools.partial(kernel, nz, ny, 111 if nz > 8 else 15 * nz + 3),
         out_shape=jax.ShapeDtypeStruct((5, 64, 512), F32),
         in_specs=[any_spec] * 9,
         out_specs=pl.BlockSpec(memory_space=pltpu.VMEM),
@@ -494,10 +625,10 @@
             pltpu.VMEM((1024, 256), F32),
             pltpu.VMEM((1024, 128), F32),
             pltpu.VMEM((5, 64, 512), F32),
-            pltpu.VMEM((8, 384), F32),
-            pltpu.VMEM((nz, 8, 384), F32),
-            pltpu.VMEM((ny, 8, 384), F32),
-            pltpu.VMEM((ny, 8, 384), F32),
+            pltpu.VMEM((8, 256), F32),
+            pltpu.VMEM((nz, 8, 256), F32),
+            pltpu.VMEM((ny, 8, 256), F32),
+            pltpu.VMEM((ny, 8, 256), F32),
             dma((9,)),
             dma((3, 7)),
             dma((3, 7)),
@@ -507,21 +638,28 @@
             dma((nz,)),
             dma((ny,)),
             dma((ny,)),
+            pltpu.SemaphoreType.REGULAR,
+            pltpu.VMEM((128, 1024), BF16),
         ],
         compiler_params=pltpu.CompilerParams(
-            collective_id=0, has_side_effects=True, vmem_limit_bytes=56 * 1024 * 1024
+            collective_id=0, has_side_effects=True, vmem_limit_bytes=40 * 1024 * 1024
         ),
         cost_estimate=pl.CostEstimate(flops=2 * 10**9, bytes_accessed=6 * 10**6, transcendentals=0),
     )(
-        flow_state[0],
-        block_owner[None],
-        link_block.T,
-        link_side.T,
-        rows_live[None],
-        x_operator,
-        ghost_operator,
-        y_operator,
-        coefficients,
+        *(
+            pltpu.with_memory_space_constraint(value, pltpu.HBM)
+            for value in (
+                flow_state[0],
+                block_owner[None],
+                link_block.T,
+                link_side.T,
+                rows_live[None],
+                x_operator,
+                ghost_operator,
+                y_operator,
+                coefficients,
+            )
+        )
     )
     return result[None]
 

time: 48.3 us -> 39.3 us (0.81)
  the two profiles are of different devices: /device:TPU:1 before, /device:TPU:8 now
where the time goes in v2:
time: 39.3 us; the launch traced here: 39.1 us
  Pallas kernels  38.3 us (97%)
  local copies, waits for them, and re-layouts  0.84 us (2%)
    pallas_call x1, Pallas kernels, on_device(): pl.pallas_call(functools.partial(kernel, nz, ny, 111 if nz > 8 else 15 *...  38.3 us
    unnamed x1, local copies, waits for them, and re-layouts  0.84 us

profile of v2, /device:TPU:8, one launch (start us, length us, event | category | flops | bytes accessed | tf_op | source)
XLA Modules:
  0.0 39.1 jit_solution(2970131724273492979)
XLA Ops:
  0.0 38.3 %shard_map.91 = f32[5,64,512]{2,1,0:T(8,128)S(1)} custom-call(f32[5,64,512]{2,1,0:T(8,128)} %bitcast.7, s32[1,128]{1,0:T(1,128)} %bitcast.10, s32[2,128]{1,0:T(2,128)} %bitcast.8, s32[2,128]{1,0:T(2,128)} %bitcast.9, s32[1,128]{1,0:T(1,128)} %bitcast.11, f32[512,1024]{1,0:T(8,128)} %xop_h.1, f32[6,1024]{1,0:T(8,128)} %gop_h.1, f32[512,1024]{1,0:T(8,128)} %yop_h.1, ...), custom_call_target="tpu_custom_call" | custom-call | flops 2000000000 | bytes 6000000 | tf_op jit(solution)/shard_map/pallas_call | solution.py:594
  38.3 0.8 %copy.11 = f32[1,5,64,512]{3,2,1,0:T(8,128)} copy(f32[1,5,64,512]{3,2,1,0:T(8,128)S(1)} %bitcast.6) | data formatting | bytes 1310720

commit v3 on v2

--- a/solution.py
+++ b/solution.py
@@ -82,61 +82,6 @@
     ready,
     gstack,
 ):
-    line = lax.axis_index("line")
-    slot = lax.axis_index("blk")
-    chip, core = line // 2, lax.rem(line, 2)
-    z, y = slot // ny, lax.rem(slot, ny)
-
-    def peer(ahead, other):
-        return lax.rem(chip + ahead, 4) * 2 + lax.rem(core + other, 2)
-
-    is_first = (slot == 0) & (line == 0)
-    late_line = (slot == 0) & (line != 0)
-    z_special = (y == 0) & (line == 0)
-    y_special = (z == 0) & (line == 0) & (y != 0)
-
-    def z_start(zz):
-        usual = jnp.where(zz < 8, 15 * zz, 88 + 4 * zz)
-        return jnp.where(z_special & (zz == 0), z_late, usual)
-
-    my_z = z_start(z)
-
-    def z_close(zz):
-        near = jnp.abs(z_start(zz) - my_z) <= 10
-        return near & jnp.logical_not(z_special & ((zz == 0) | (z == 0)))
-
-    def z_now(zz):
-        return (zz != z) & ((z_start(zz) < my_z) | z_close(zz))
-
-    def z_after(zz, least, most):
-        gap = z_start(zz) - my_z
-        return (gap > least) & (gap <= most) & jnp.logical_not(z_close(zz))
-
-    barrier = pltpu.get_barrier_semaphore()
-
-    @pl.when(jnp.logical_not(is_first))
-    def _():
-        for ahead, other in PEERS:
-            pl.semaphore_signal(
-                barrier, inc=1, device_id={"line": peer(ahead, other)}, device_id_type=MESH
-            )
-
-    waits = len(PEERS) - jnp.where(late_line, 1, 0) + ny - 1 - jnp.where(y_special, 1, 0)
-    for zz in range(nz):
-        waits += jnp.where(z_now(zz), 1, 0)
-
-    @pl.loop(0, nz)
-    def _(zz):
-        @pl.when((zz != z) & ((z_start(zz) > my_z) | z_close(zz)))
-        def _():
-            pl.semaphore_signal(barrier, inc=1, device_id={"blk": zz * ny + y}, device_id_type=MESH)
-
-    @pl.loop(0, ny)
-    def _(yy):
-        @pl.when((yy != y) & jnp.logical_not(is_first))
-        def _():
-            pl.semaphore_signal(barrier, inc=1, device_id={"blk": z * ny + yy}, device_id_type=MESH)
-
     loads = [
         pltpu.make_async_copy(a, b, load_sem.at[i])
         for i, (a, b) in enumerate(
@@ -155,6 +100,55 @@
     ]
     for load in loads:
         load.start()
+
+    line = lax.axis_index("line")
+    slot = lax.axis_index("blk")
+    chip, core = line // 2, lax.rem(line, 2)
+    z, y = slot // ny, lax.rem(slot, ny)
+
+    def peer(ahead, other):
+        return lax.rem(chip + ahead, 4) * 2 + lax.rem(core + other, 2)
+
+    is_first = (slot == 0) & (line == 0)
+    late_line = (slot == 0) & (line != 0)
+    z_special = (y == 0) & (line == 0)
+    y_special = (z == 0) & (line == 0) & (y != 0)
+
+    def usual(zz):
+        return jnp.where(zz < 8, 15 * zz, 88 + 4 * zz)
+
+    my_z = jnp.where(is_first, z_late, usual(z))
+    gaps = [jnp.where(z_special, z_late, 0) - my_z]
+    gaps += [(15 * zz if zz < 8 else 88 + 4 * zz) - my_z for zz in range(1, nz)]
+    close = [jnp.abs(gap) <= 10 for gap in gaps]
+    close[0] = close[0] & jnp.logical_not(z_special)
+    close = [here & jnp.logical_not(is_first) for here in close]
+    now = [(z != zz) & ((gaps[zz] < 0) | close[zz]) for zz in range(nz)]
+
+    barrier = pltpu.get_barrier_semaphore()
+
+    @pl.when(jnp.logical_not(is_first))
+    def _():
+        for ahead, other in PEERS:
+            pl.semaphore_signal(
+                barrier, inc=1, device_id={"line": peer(ahead, other)}, device_id_type=MESH
+            )
+
+    waits = len(PEERS) - jnp.where(late_line, 1, 0) + ny - 1 - jnp.where(y_special, 1, 0)
+    for zz in range(nz):
+        waits += jnp.where(now[zz], 1, 0)
+
+    for zz in range(nz):
+
+        @pl.when((z != zz) & ((gaps[zz] > 0) | close[zz]))
+        def _():
+            pl.semaphore_signal(barrier, inc=1, device_id={"blk": zz * ny + y}, device_id_type=MESH)
+
+    for yy in range(ny):
+
+        @pl.when((y != yy) & jnp.logical_not(is_first))
+        def _():
+            pl.semaphore_signal(barrier, inc=1, device_id={"blk": z * ny + yy}, device_id_type=MESH)
 
     @pl.when(is_first)
     def _():
@@ -275,13 +269,24 @@
         def _():
             forward(chunk, i).start()
 
-    @pl.loop(0, nz)
-    def _(zz):
-        @pl.when(z_now(zz))
+    @pl.when(is_first)
+    def _():
+        for i in range(7):
+            forward(0, i).start()
+
+    for zz in range(nz):
+
+        @pl.when(now[zz])
         def _():
             z_copy(zz, z).start()
 
-    for chunk in range(3):
+    for i in range(7):
+
+        @pl.when(jnp.logical_not(is_first | is_late(i)))
+        def _():
+            forward(0, i).start()
+
+    for chunk in (1, 2):
         for i in range(7):
             send_forward(chunk, i)
 
@@ -317,7 +322,12 @@
             jnp.where(hot, link_side_v[side : side + 1, :].astype(F32), 0.0), axis=1, keepdims=True
         )
         source = jnp.sum(jnp.where(lane_row == partner, owner_f, 0.0), axis=1, keepdims=True)
-        wanted.append((source, far))
+        source = source.astype(jnp.int32)
+        source_z = source // ny
+        bits = []
+        while 2 ** len(bits) < nz:
+            bits.append((source_z // 2 ** len(bits) % 2).astype(F32))
+        wanted.append((bits, far, (source % ny == y).astype(F32)))
 
     own = []
     for side in range(2):
@@ -340,34 +350,48 @@
         for f in range(2)
     ]
 
-    def answer(least, most):
-        @pl.loop(1, nz + 1)
-        def _(step):
-            zz = lax.rem(step, nz)
-
-            @pl.when(z_after(zz, least, most))
+    def between(zz, least, most):
+        return (gaps[zz] > least) & (gaps[zz] <= most) & jnp.logical_not(close[zz])
+
+    order = (*range(1, min(8, nz)), 0, *range(8, nz))
+
+    def answer(least, most, first_most=None):
+        for zz in order:
+
+            @pl.when(between(zz, least, most if zz or first_most is None else first_most))
             def _():
                 z_copy(zz, zz).wait_recv()
                 z_copy(zz, z).start()
 
     def ghost_stage():
-        answer(60, 1000)
-
-        @pl.loop(0, nz)
-        def _(zz):
-            @pl.when(z_now(zz))
+        for zz in range(1, nz):
+
+            @pl.when(between(zz, 45, 1000))
+            def _():
+                z_copy(zz, zz).wait_recv()
+
+            @pl.when(between(zz, 45, 80))
+            def _():
+                z_copy(zz, z).start()
+
+        for zz in range(nz):
+
+            @pl.when(now[zz])
             def _():
                 z_copy(zz, zz).wait_recv()
 
         for p in range(ny):
             message = jnp.zeros((8, 256), F32)
             for side in range(2):
-                source = jnp.broadcast_to(wanted[side][0][p : p + 1], (8, 256))
                 far = jnp.broadcast_to(wanted[side][1][p : p + 1], (8, 256))
-                total = jnp.zeros((8, 256), F32)
-                for zz in range(nz):
-                    code = (y + zz * ny).astype(F32)
-                    total = total + jnp.where(source == code, gz[zz], 0.0)
+                level = [gz[zz] for zz in range(nz)]
+                for bits in wanted[side][0]:
+                    bit = jnp.broadcast_to(bits[p : p + 1], (8, 256)) > 0.5
+                    level = [
+                        jnp.where(bit, level[k + 1], level[k]) for k in range(0, len(level), 2)
+                    ]
+                inside = jnp.broadcast_to(wanted[side][2][p : p + 1], (8, 256)) > 0.5
+                total = jnp.where(inside, level[0], 0.0)
                 halves = jnp.concatenate(
                     [pltpu.roll(total[:, 128 * j : 128 * j + 128], 64, 1) for j in range(2)], axis=1
                 )
@@ -380,11 +404,17 @@
         def _():
             pl.semaphore_wait(ready, 1)
 
-        @pl.loop(0, ny)
-        def _(yy):
-            @pl.when(yy != y)
+        for yy in range(ny):
+
+            @pl.when(y != yy)
             def _():
                 y_copy(yy, y).start()
+
+        for zz in range(1, nz):
+
+            @pl.when(between(zz, 80, 1000))
+            def _():
+                z_copy(zz, z).start()
 
         ry[y] = sy[y]
 
@@ -424,7 +454,7 @@
     lo_all = lax.broadcasted_iota(jnp.int32, (512, 128), 1) < 64
     vv[...] = STEP * jnp.where(lo_all, start, pltpu.roll(start, 64, 1))
     y_pair(0, nu[1], nu[0])
-    answer(0, 30)
+    answer(0, 20, 20)
     for i in range(7):
         backward(0, i).start()
     b_ab[0, line] = t_ab[0, here]
@@ -432,7 +462,7 @@
     for i in range(7):
         forward(1, i).wait_recv()
     y_pair(1, nu[2], nu[3])
-    answer(30, 60)
+    answer(20, 45, 1000)
     for i in range(7):
         backward(1, i).start()
     b_ab[1, line] = t_ab[1, here]
@@ -461,6 +491,7 @@
     for i in range(7):
         backward(2, i).start()
     b_c[line] = t_c[line]
+    pl.when(is_first)(ghost_stage)
 
     loads[8].wait()
 
@@ -493,7 +524,7 @@
                 term = term + (STEP * coef[5]) * m[3, :, cols] + (STEP * coef[6]) * m[4, :, cols]
             acc[v, :, cols] = term
 
-    ghost_stage()
+    pl.when(jnp.logical_not(is_first))(ghost_stage)
 
     for pair, (first, second) in enumerate(((1, 0), (2, 3))):
         for i in range(7):
@@ -504,11 +535,28 @@
             acc[first, :, cols] += jnp.where(lo, a, pltpu.roll(b, 64, 1))
             acc[second, :, cols] += jnp.where(lo, pltpu.roll(a, 64, 1), b)
 
-    @pl.loop(0, ny)
-    def _(yy):
-        @pl.when(yy != y)
+    for chunk in range(3):
+        for i in range(7):
+            forward(chunk, i).wait_send()
+            if chunk < 2:
+                backward(chunk, i).wait_send()
+    for zz in range(nz):
+
+        @pl.when(z != zz)
+        def _():
+            z_copy(zz, z).wait_send()
+
+    for yy in range(ny):
+
+        @pl.when(y != yy)
         def _():
             y_copy(yy, yy).wait_recv()
+
+    for yy in range(ny):
+
+        @pl.when(y != yy)
+        def _():
+            y_copy(yy, y).wait_send()
 
     ghost = ry[0]
     for p in range(1, ny):
@@ -557,22 +605,8 @@
         out[4, :32, cols] = live[:32] * (acc[4, :32, cols] + top)
         out[4, 32:, cols] = live[32:] * (acc[4, 32:, cols] + bottom)
 
-    for chunk in range(3):
-        for i in range(7):
-            forward(chunk, i).wait_send()
-            backward(chunk, i).wait_send()
-
-    @pl.loop(0, nz)
-    def _(zz):
-        @pl.when(zz != z)
-        def _():
-            z_copy(zz, z).wait_send()
-
-    @pl.loop(0, ny)
-    def _(yy):
-        @pl.when(yy != y)
-        def _():
-            y_copy(yy, y).wait_send()
+    for i in range(7):
+        backward(2, i).wait_send()
 
 
 def on_device(

time: 39.3 us -> 36.6 us (0.931)
  Pallas kernels: 38.3 us -> 35.6 us
    pallas_call x1, Pallas kernels: 38.3 us -> 35.6 us  [on_device(): pl.pallas_call(functools.partial(kernel, nz, ny, 111 if nz > 8 else 15 *...]
where the time goes in v3:
time: 36.6 us; the launch traced here: 36.5 us
  Pallas kernels  35.6 us (97%)
  local copies, waits for them, and re-layouts  0.84 us (2%)
    pallas_call x1, Pallas kernels, on_device(): pl.pallas_call(functools.partial(kernel, nz, ny, 111 if nz > 8 else 15 *...  35.6 us
    unnamed x1, local copies, waits for them, and re-layouts  0.84 us

profile of v3, /device:TPU:8, one launch (start us, length us, event | category | flops | bytes accessed | tf_op | source)
XLA Modules:
  0.0 36.5 jit_solution(3474247515891593578)
XLA Ops:
  0.0 35.6 %shard_map.91 = f32[5,64,512]{2,1,0:T(8,128)S(1)} custom-call(f32[5,64,512]{2,1,0:T(8,128)} %bitcast.7, s32[1,128]{1,0:T(1,128)} %bitcast.10, s32[2,128]{1,0:T(2,128)} %bitcast.8, s32[2,128]{1,0:T(2,128)} %bitcast.9, s32[1,128]{1,0:T(1,128)} %bitcast.11, f32[512,1024]{1,0:T(8,128)} %xop_h.1, f32[6,1024]{1,0:T(8,128)} %gop_h.1, f32[512,1024]{1,0:T(8,128)} %yop_h.1, ...), custom_call_target="tpu_custom_call" | custom-call | flops 2000000000 | bytes 6000000 | tf_op jit(solution)/shard_map/pallas_call | solution.py:628
  35.6 0.8 %copy.11 = f32[1,5,64,512]{3,2,1,0:T(8,128)} copy(f32[1,5,64,512]{3,2,1,0:T(8,128)S(1)} %bitcast.6) | data formatting | bytes 1310720

commit v4 on v3

--- a/solution.py
+++ b/solution.py
@@ -173,26 +173,10 @@
     live = (row_id < live_rows).astype(F32)
     loads[2].wait()
 
-    for pair, (first, second) in enumerate(((1, 0), (2, 3))):
-        for c in range(4):
-            cols = slice(128 * c, 128 * c + 128)
-            a = m[first, :, cols] * live
-            b = m[second, :, cols] * live
-            m[first, :, cols] = a
-            m[second, :, cols] = b
-            s_ab[pair, 2 * c] = jnp.where(lo, a, pltpu.roll(b, 64, 1))
-            s_ab[pair, 2 * c + 1] = jnp.where(lo, pltpu.roll(a, 64, 1), b)
-    lo32 = lo[:32]
-    for c in range(4):
-        cols = slice(128 * c, 128 * c + 128)
-        a = m[4, :, cols] * live
-        m[4, :, cols] = a
-        s_c[2 * c] = jnp.where(lo32, a[:32], pltpu.roll(a[32:], 64, 1))
-        s_c[2 * c + 1] = jnp.where(lo32, pltpu.roll(a[:32], 64, 1), a[32:])
-
     planes = []
     for v in range(5):
-        planes.append(jnp.where(lanes < 3, m[v, :, 0:128], pltpu.roll(m[v, :, 384:512], 6, 1)))
+        low, high = m[v, :, 0:128], pltpu.roll(m[v, :, 384:512], 6, 1)
+        planes.append(live * jnp.where(lanes < 3, low, high))
     last = planes[4]
     for v, moves in enumerate(((6, 6), (3, 3), (4, None), (1, None))):
         for lane, move in zip((6, 7), moves):
@@ -269,26 +253,42 @@
         def _():
             forward(chunk, i).start()
 
-    @pl.when(is_first)
-    def _():
-        for i in range(7):
-            forward(0, i).start()
-
     for zz in range(nz):
 
-        @pl.when(now[zz])
+        @pl.when(now[zz] if zz < 8 else now[zz] & (z < 8))
         def _():
             z_copy(zz, z).start()
 
-    for i in range(7):
-
-        @pl.when(jnp.logical_not(is_first | is_late(i)))
-        def _():
-            forward(0, i).start()
-
-    for chunk in (1, 2):
-        for i in range(7):
-            send_forward(chunk, i)
+    def pack(pair, first, second):
+        for c in range(4):
+            cols = slice(128 * c, 128 * c + 128)
+            a = m[first, :, cols] * live
+            b = m[second, :, cols] * live
+            m[first, :, cols] = a
+            m[second, :, cols] = b
+            s_ab[pair, 2 * c] = jnp.where(lo, a, pltpu.roll(b, 64, 1))
+            s_ab[pair, 2 * c + 1] = jnp.where(lo, pltpu.roll(a, 64, 1), b)
+    pack(0, 1, 0)
+    for i in range(7):
+        send_forward(0, i)
+    pack(1, 2, 3)
+    for i in range(7):
+        send_forward(1, i)
+    lo32 = lo[:32]
+    for c in range(4):
+        cols = slice(128 * c, 128 * c + 128)
+        a = m[4, :, cols] * live
+        m[4, :, cols] = a
+        s_c[2 * c] = jnp.where(lo32, a[:32], pltpu.roll(a[32:], 64, 1))
+        s_c[2 * c + 1] = jnp.where(lo32, pltpu.roll(a[:32], 64, 1), a[32:])
+
+    for i in range(7):
+        send_forward(2, i)
+    for zz in range(8, nz):
+
+        @pl.when(now[zz] & (z >= 8))
+        def _():
+            z_copy(zz, z).start()
 
     gz[z] = face[...]
     r_ab[0, here] = s_ab[0, line]
@@ -355,22 +355,22 @@
 
     order = (*range(1, min(8, nz)), 0, *range(8, nz))
 
-    def answer(least, most, first_most=None):
+    def answer(least, most, first_least, first_most):
         for zz in order:
 
-            @pl.when(between(zz, least, most if zz or first_most is None else first_most))
+            @pl.when(between(zz, least, most) if zz else between(zz, first_least, first_most))
             def _():
                 z_copy(zz, zz).wait_recv()
                 z_copy(zz, z).start()
 
-    def ghost_stage():
+    def ghost_stage(least=45):
         for zz in range(1, nz):
 
-            @pl.when(between(zz, 45, 1000))
+            @pl.when(between(zz, least, 1000))
             def _():
                 z_copy(zz, zz).wait_recv()
 
-            @pl.when(between(zz, 45, 80))
+            @pl.when(between(zz, least, 80))
             def _():
                 z_copy(zz, z).start()
 
@@ -454,7 +454,7 @@
     lo_all = lax.broadcasted_iota(jnp.int32, (512, 128), 1) < 64
     vv[...] = STEP * jnp.where(lo_all, start, pltpu.roll(start, 64, 1))
     y_pair(0, nu[1], nu[0])
-    answer(0, 20, 20)
+    answer(0, 20, 0, 40)
     for i in range(7):
         backward(0, i).start()
     b_ab[0, line] = t_ab[0, here]
@@ -462,7 +462,7 @@
     for i in range(7):
         forward(1, i).wait_recv()
     y_pair(1, nu[2], nu[3])
-    answer(20, 45, 1000)
+    pl.when(jnp.logical_not(is_first))(lambda: answer(20, 45, 40, 1000))
     for i in range(7):
         backward(1, i).start()
     b_ab[1, line] = t_ab[1, here]
@@ -491,7 +491,7 @@
     for i in range(7):
         backward(2, i).start()
     b_c[line] = t_c[line]
-    pl.when(is_first)(ghost_stage)
+    pl.when(is_first)(lambda: ghost_stage(20))
 
     loads[8].wait()
 

time: 36.6 us -> 35.9 us (0.981)
  Pallas kernels: 35.6 us -> 35 us
    pallas_call x1, Pallas kernels: 35.6 us -> 35 us  [on_device(): pl.pallas_call(functools.partial(kernel, nz, ny, 111 if nz > 8 else 15 *...]
where the time goes in v4:
time: 35.9 us; the launch traced here: 35.8 us
  Pallas kernels  35 us (97%)
  local copies, waits for them, and re-layouts  0.84 us (2%)
    pallas_call x1, Pallas kernels, on_device(): pl.pallas_call(functools.partial(kernel, nz, ny, 111 if nz > 8 else 15 *...  35 us
    unnamed x1, local copies, waits for them, and re-layouts  0.84 us

profile of v4, /device:TPU:8, one launch (start us, length us, event | category | flops | bytes accessed | tf_op | source)
XLA Modules:
  0.0 35.8 jit_solution(28158874293150045)
XLA Ops:
  0.0 35.0 %shard_map.91 = f32[5,64,512]{2,1,0:T(8,128)S(1)} custom-call(f32[5,64,512]{2,1,0:T(8,128)} %bitcast.7, s32[1,128]{1,0:T(1,128)} %bitcast.10, s32[2,128]{1,0:T(2,128)} %bitcast.8, s32[2,128]{1,0:T(2,128)} %bitcast.9, s32[1,128]{1,0:T(1,128)} %bitcast.11, f32[512,1024]{1,0:T(8,128)} %xop_h.1, f32[6,1024]{1,0:T(8,128)} %gop_h.1, f32[512,1024]{1,0:T(8,128)} %yop_h.1, ...), custom_call_target="tpu_custom_call" | custom-call | flops 2000000000 | bytes 6000000 | tf_op jit(solution)/shard_map/pallas_call | solution.py:628
  35.0 0.8 %copy.11 = f32[1,5,64,512]{3,2,1,0:T(8,128)} copy(f32[1,5,64,512]{3,2,1,0:T(8,128)S(1)} %bitcast.6) | data formatting | bytes 1310720

commit v5 on v4

--- a/solution.py
+++ b/solution.py
@@ -535,28 +535,11 @@
             acc[first, :, cols] += jnp.where(lo, a, pltpu.roll(b, 64, 1))
             acc[second, :, cols] += jnp.where(lo, pltpu.roll(a, 64, 1), b)
 
-    for chunk in range(3):
-        for i in range(7):
-            forward(chunk, i).wait_send()
-            if chunk < 2:
-                backward(chunk, i).wait_send()
-    for zz in range(nz):
-
-        @pl.when(z != zz)
-        def _():
-            z_copy(zz, z).wait_send()
-
     for yy in range(ny):
 
         @pl.when(y != yy)
         def _():
             y_copy(yy, yy).wait_recv()
-
-    for yy in range(ny):
-
-        @pl.when(y != yy)
-        def _():
-            y_copy(yy, y).wait_send()
 
     ghost = ry[0]
     for p in range(1, ny):
@@ -604,6 +587,23 @@
         bottom = jnp.where(lo32, pltpu.roll(a, 64, 1), b)
         out[4, :32, cols] = live[:32] * (acc[4, :32, cols] + top)
         out[4, 32:, cols] = live[32:] * (acc[4, 32:, cols] + bottom)
+
+    for chunk in range(3):
+        for i in range(7):
+            forward(chunk, i).wait_send()
+            if chunk < 2:
+                backward(chunk, i).wait_send()
+    for zz in range(nz):
+
+        @pl.when(z != zz)
+        def _():
+            z_copy(zz, z).wait_send()
+
+    for yy in range(ny):
+
+        @pl.when(y != yy)
+        def _():
+            y_copy(yy, y).wait_send()
 
     for i in range(7):
         backward(2, i).wait_send()

time: 35.9 us -> 36 us (level)
  no operation moved by 1% of the time
where the time goes in v5:
time: 36 us; the launch traced here: 35.9 us
  Pallas kernels  35 us (97%)
  local copies, waits for them, and re-layouts  0.84 us (2%)
    pallas_call x1, Pallas kernels, on_device(): pl.pallas_call(functools.partial(kernel, nz, ny, 111 if nz > 8 else 15 *...  35 us
    unnamed x1, local copies, waits for them, and re-layouts  0.84 us

profile of v5, /device:TPU:8, one launch (start us, length us, event | category | flops | bytes accessed | tf_op | source)
XLA Modules:
  0.0 35.9 jit_solution(8732406556490638293)
XLA Ops:
  0.0 35.0 %shard_map.91 = f32[5,64,512]{2,1,0:T(8,128)S(1)} custom-call(f32[5,64,512]{2,1,0:T(8,128)} %bitcast.7, s32[1,128]{1,0:T(1,128)} %bitcast.10, s32[2,128]{1,0:T(2,128)} %bitcast.8, s32[2,128]{1,0:T(2,128)} %bitcast.9, s32[1,128]{1,0:T(1,128)} %bitcast.11, f32[512,1024]{1,0:T(8,128)} %xop_h.1, f32[6,1024]{1,0:T(8,128)} %gop_h.1, f32[512,1024]{1,0:T(8,128)} %yop_h.1, ...), custom_call_target="tpu_custom_call" | custom-call | flops 2000000000 | bytes 6000000 | tf_op jit(solution)/shard_map/pallas_call | solution.py:628
  35.0 0.8 %copy.11 = f32[1,5,64,512]{3,2,1,0:T(8,128)} copy(f32[1,5,64,512]{3,2,1,0:T(8,128)S(1)} %bitcast.6) | data formatting | bytes 1310720
